TPU v7x, 32 devices: a whole 2x2x4 slice. The times are simulated.
32 devices in a mesh: dp: 4 (over y, x), seq: 8 (over z, core).
Axes of the slice: x: 2, y: 2, z: 4, core: 2. Of those that a mesh axis runs over, the one named last changes fastest.
Arguments:
- inputs: bfloat16 [8, 1024, 768], P('dp', 'seq'), may hold values from -6 to 6
- memory: bfloat16 [8, 1024, 768], P('dp', 'seq'), may hold values from -6 to 6
- cotangent: bfloat16 [8, 1024, 768], P('dp', 'seq'), may hold values from -6 to 6
- segment_ids: int32 [8, 1024], P('dp', 'seq'), may hold values from 0 to 3, never falling along the last dimension, each value on 1 to 512 neighbouring positions
- row_live: int32 [8], P('dp'), may hold values 0 or 1
- buckets: int32 [1024], replicated, may hold values from 0 to 31, as said below
- gain_self: bfloat16 [768], P('dp'), may hold values from 0.5 to 1.5
- w_qkv: bfloat16 [768, 2304], P('dp'), may hold values from -0.21875 to 0.21875
- w_attn_out: bfloat16 [768, 768], P('dp'), may hold values from -2 to 2
- rel_bias: bfloat16 [32, 12], P('dp'), may hold values from -4 to 4
- gain_cross: bfloat16 [768], P('dp'), may hold values from 0.5 to 1.5
- c_query: bfloat16 [768, 768], P('dp'), may hold values from -0.21875 to 0.21875
- c_keyval: bfloat16 [768, 1536], P('dp'), may hold values from -0.21875 to 0.21875
- c_out: bfloat16 [768, 768], P('dp'), may hold values from -2 to 2
- gain_ff: bfloat16 [768], P('dp'), may hold values from 0.5 to 1.5
- w_gate_up: bfloat16 [768, 4096], P('dp'), may hold values from -0.21875 to 0.21875
- w_down: bfloat16 [2048, 768], P('dp'), may hold values from -0.125 to 0.125
Outputs:
- output: bfloat16 [8, 1024, 768], P('dp', 'seq')
- grad_inputs: bfloat16 [8, 1024, 768], P('dp', 'seq')
- grad_memory: bfloat16 [8, 1024, 768], P('dp', 'seq')
- grad_gain_self: float32 [768], P('dp')
- grad_w_qkv: float32 [768, 2304], P('dp')
- grad_w_attn_out: float32 [768, 768], P('dp')
- grad_rel_bias: float32 [32, 12], P('dp')
- grad_gain_cross: float32 [768], P('dp')
- grad_c_query: float32 [768, 768], P('dp')
- grad_c_keyval: float32 [768, 1536], P('dp')
- grad_c_out: float32 [768, 768], P('dp')
- grad_gain_ff: float32 [768], P('dp')
- grad_w_gate_up: float32 [768, 4096], P('dp')
- grad_w_down: float32 [2048, 768], P('dp')
Inputs may be any that keep to these rules, and one draw needn't show every extreme that they name: `segment_ids`: along each row the segment ids never fall; every row holds all 4 segments. buckets[d] never falls as the distance d grows, is 0 at d = 0 and reaches 31.
All inputs are finite; a program needn't handle non-finite values. No bound on the sum of `row_live` on one device may be relied on, other than what follows from the above.
Results may differ from a plain program's by a relative error of at most 0.029.
Values may be sent and summed in bfloat16 or wider, within the bound.
A program may use at most 192 MiB of HBM per device.

v0:
```python
import jax
import jax.numpy as jnp
from jax import lax
from jax.sharding import PartitionSpec as P

D = 768
HEADS = 12
HEAD_DIM = 64
FF = 2048
BUCKETS = 32
LEN = 1024
MEM = 1024


epsilon = 1e-06
masked_score = -1000000000.0
highest = lax.Precision.HIGHEST


def rms_norm(values, gain):
    return values * lax.rsqrt(jnp.mean(values * values, axis=-1, keepdims=True) + epsilon) * gain


def matmul(left, right, form):
    return jnp.einsum(form, left, right, preferred_element_type=jnp.float32)


def softmax_parts(scores):
    top = jnp.max(scores, axis=-1, keepdims=True)
    expo = jnp.exp(scores - top)
    total = jnp.sum(expo, axis=-1, keepdims=True)
    return (expo / total, (top + jnp.log(total))[..., 0])


def score_grads(scores, lse_row, value_row, grad_row):
    probs = jnp.exp(scores - lse_row[..., None])
    grad_probs = matmul(grad_row, value_row, "qhd,khd->hqk")
    centre = jnp.sum(grad_probs * probs, axis=-1, keepdims=True)
    grad_scores = (probs * (grad_probs - centre)).astype(jnp.bfloat16)
    return (probs, grad_scores, centre[..., 0])


def bucket_mask(buckets, offsets):
    bucket_of = jnp.take(buckets, jnp.clip(offsets, 0, LEN - 1), axis=0)
    return (bucket_of[..., None] == jnp.arange(BUCKETS, dtype=jnp.int32)).astype(jnp.float32)


def bias_from(table, mask):
    return jnp.einsum(
        "qkb,bh->hqk", mask, table, precision=highest, preferred_element_type=jnp.float32
    )


def per_device(
    inputs,
    memory,
    cotangent,
    segment_ids,
    row_live,
    buckets,
    gain_self,
    w_qkv,
    w_attn_out,
    rel_bias,
    gain_cross,
    c_query,
    c_keyval,
    c_out,
    gain_ff,
    w_gate_up,
    w_down,
):
    (
        g_self,
        qkv_full,
        out_full,
        bias_full,
        g_cross,
        cq_full,
        ckv_full,
        cout_full,
        g_ffn,
        gu_full,
        down_full,
    ) = (
        lax.all_gather(gain_self, "dp", axis=0, tiled=True),
        lax.all_gather(w_qkv, "dp", axis=0, tiled=True),
        lax.all_gather(w_attn_out, "dp", axis=0, tiled=True),
        lax.all_gather(rel_bias, "dp", axis=0, tiled=True),
        lax.all_gather(gain_cross, "dp", axis=0, tiled=True),
        lax.all_gather(c_query, "dp", axis=0, tiled=True),
        lax.all_gather(c_keyval, "dp", axis=0, tiled=True),
        lax.all_gather(c_out, "dp", axis=0, tiled=True),
        lax.all_gather(gain_ff, "dp", axis=0, tiled=True),
        lax.all_gather(w_gate_up, "dp", axis=0, tiled=True),
        lax.all_gather(w_down, "dp", axis=0, tiled=True),
    )
    num_rows, local_len, _ = inputs.shape
    seq_index = lax.axis_index("seq")
    scale = HEAD_DIM ** (-0.5)
    dense = inputs.astype(jnp.float32)
    live_rows = row_live.astype(jnp.float32)[:, None, None]
    normed_one = rms_norm(dense, g_self.astype(jnp.float32))
    hidden_one = normed_one.astype(jnp.bfloat16)
    qkv_local = matmul(hidden_one, qkv_full, "rcd,de->rce").astype(jnp.bfloat16)
    queries = qkv_local[..., :D]
    key_value = qkv_local[..., D:]
    seg_local = segment_ids.astype(jnp.bfloat16)
    key_all, seg_all = (
        lax.all_gather(key_value, "seq", axis=1, tiled=True),
        lax.all_gather(seg_local, "seq", axis=1, tiled=True),
    )
    positions = seq_index * local_len + jnp.arange(local_len, dtype=jnp.int32)
    offsets = positions[:, None] - jnp.arange(LEN, dtype=jnp.int32)[None, :]
    causal = offsets >= 0
    self_mask = bucket_mask(buckets, offsets)
    bias_block = bias_from(bias_full.astype(jnp.float32), self_mask)

    def self_scores(queries_h, key_row, seg_row, segk_row):
        raw = matmul(queries_h, key_row, "qhd,khd->hqk") * scale + bias_block
        allowed = causal & (seg_row[:, None] == segk_row[None, :])
        return jnp.where(allowed[None], raw, masked_score)

    def self_forward(items):
        query_row, kv_row, seg_row, segk_row = items
        key_row = kv_row[:, :D].reshape(LEN, HEADS, HEAD_DIM)
        value_row = kv_row[:, D:].reshape(LEN, HEADS, HEAD_DIM)
        scores = self_scores(
            query_row.reshape(local_len, HEADS, HEAD_DIM), key_row, seg_row, segk_row
        )
        probs, lse_row = softmax_parts(scores)
        mixed = matmul(probs.astype(jnp.bfloat16), value_row, "hqk,khd->qhd")
        return (mixed.reshape(local_len, D), lse_row)

    attn_self, lse_self = lax.map(self_forward, (queries, key_all, seg_local, seg_all))
    attn_low = attn_self.astype(jnp.bfloat16)
    branch_one = matmul(attn_low, out_full, "rcd,de->rce")
    after_self = dense + live_rows * branch_one
    normed_two = rms_norm(after_self, g_cross.astype(jnp.float32))
    hidden_two = normed_two.astype(jnp.bfloat16)
    cross_q = matmul(hidden_two, cq_full, "rcd,de->rce").astype(jnp.bfloat16)
    memory_kv = matmul(memory, ckv_full, "rmd,de->rme").astype(jnp.bfloat16)
    memory_all = lax.all_gather(memory_kv, "seq", axis=1, tiled=True)

    def cross_forward(items):
        query_row, kv_row = items
        key_row = kv_row[:, :D].reshape(MEM, HEADS, HEAD_DIM)
        value_row = kv_row[:, D:].reshape(MEM, HEADS, HEAD_DIM)
        scores = (
            matmul(query_row.reshape(local_len, HEADS, HEAD_DIM), key_row, "qhd,khd->hqk") * scale
        )
        probs, lse_row = softmax_parts(scores)
        mixed = matmul(probs.astype(jnp.bfloat16), value_row, "hqk,khd->qhd")
        return (mixed.reshape(local_len, D), lse_row)

    attn_cross, lse_cross = lax.map(cross_forward, (cross_q, memory_all))
    cross_low = attn_cross.astype(jnp.bfloat16)
    branch_two = matmul(cross_low, cout_full, "rcd,de->rce")
    after_cross = after_self + live_rows * branch_two
    normed_three = rms_norm(after_cross, g_ffn.astype(jnp.float32))
    hidden_three = normed_three.astype(jnp.bfloat16)
    gate_up = matmul(hidden_three, gu_full, "rcd,df->rcf")
    gate = gate_up[..., :FF]
    upward = gate_up[..., FF:]
    mixed_ff = (jax.nn.gelu(gate, approximate=True) * upward).astype(jnp.bfloat16)
    branch_three = matmul(mixed_ff, down_full, "rcf,fd->rcd")
    output = (after_cross + live_rows * branch_three).astype(jnp.bfloat16)
    (
        g_self,
        qkv_full,
        out_full,
        bias_full,
        g_cross,
        cq_full,
        ckv_full,
        cout_full,
        g_ffn,
        gu_full,
        down_full,
    ) = (
        lax.all_gather(gain_self, "dp", axis=0, tiled=True),
        lax.all_gather(w_qkv, "dp", axis=0, tiled=True),
        lax.all_gather(w_attn_out, "dp", axis=0, tiled=True),
        lax.all_gather(rel_bias, "dp", axis=0, tiled=True),
        lax.all_gather(gain_cross, "dp", axis=0, tiled=True),
        lax.all_gather(c_query, "dp", axis=0, tiled=True),
        lax.all_gather(c_keyval, "dp", axis=0, tiled=True),
        lax.all_gather(c_out, "dp", axis=0, tiled=True),
        lax.all_gather(gain_ff, "dp", axis=0, tiled=True),
        lax.all_gather(w_gate_up, "dp", axis=0, tiled=True),
        lax.all_gather(w_down, "dp", axis=0, tiled=True),
    )
    grad_out = cotangent.astype(jnp.float32)
    down_in = (live_rows * grad_out).astype(jnp.bfloat16)
    grad_down = matmul(mixed_ff, down_in, "rcf,rcd->fd")
    grad_mixed = matmul(down_in, down_full, "rcd,fd->rcf")
    _, gelu_pull = jax.vjp(
        lambda gate_in, up_in: jax.nn.gelu(gate_in, approximate=True) * up_in, gate, upward
    )
    grad_gate, grad_upward = gelu_pull(grad_mixed)
    grad_gu_low = jnp.concatenate([grad_gate, grad_upward], axis=-1).astype(jnp.bfloat16)
    grad_gate_up = matmul(hidden_three, grad_gu_low, "rcd,rcf->df")
    grad_normed_three = matmul(grad_gu_low, gu_full, "rcf,df->rcd")
    _, pull_three = jax.vjp(rms_norm, after_cross, g_ffn.astype(jnp.float32))
    part_three, grad_gain_ff = pull_three(grad_normed_three)
    grad_after_cross = grad_out + part_three
    cross_in = (live_rows * grad_after_cross).astype(jnp.bfloat16)
    grad_cout = matmul(cross_low, cross_in, "rcd,rce->de")
    grad_cross_attn = matmul(cross_in, cout_full, "rce,de->rcd").astype(jnp.bfloat16)

    def cross_backward(items):
        query_row, kv_row, lse_row, grad_row = items
        queries_h = query_row.reshape(local_len, HEADS, HEAD_DIM)
        grad_h = grad_row.reshape(local_len, HEADS, HEAD_DIM)
        key_row = kv_row[:, :D].reshape(MEM, HEADS, HEAD_DIM)
        value_row = kv_row[:, D:].reshape(MEM, HEADS, HEAD_DIM)
        scores = matmul(queries_h, key_row, "qhd,khd->hqk") * scale
        probs, grad_scores, centre = score_grads(scores, lse_row, value_row, grad_h)
        grad_query = matmul(grad_scores, key_row, "hqk,khd->qhd") * scale
        grad_key = matmul(grad_scores, queries_h, "hqk,qhd->khd") * scale
        grad_value = matmul(probs.astype(jnp.bfloat16), grad_h, "hqk,qhd->khd")
        kv_grads = jnp.concatenate([grad_key.reshape(MEM, D), grad_value.reshape(MEM, D)], axis=-1)
        return (grad_query.reshape(local_len, D), kv_grads, centre)

    grad_cq_rows, grad_memkv_full, _ = lax.map(
        cross_backward, (cross_q, memory_all, lse_cross, grad_cross_attn)
    )
    grad_memkv = lax.psum_scatter(
        grad_memkv_full.astype(jnp.bfloat16), "seq", scatter_dimension=1, tiled=True
    )
    grad_ckv = matmul(memory, grad_memkv, "rmd,rme->de")
    grad_memory = matmul(grad_memkv, ckv_full, "rme,de->rmd").astype(jnp.bfloat16)
    grad_cq_low = grad_cq_rows.astype(jnp.bfloat16)
    grad_cquery = matmul(hidden_two, grad_cq_low, "rcd,rce->de")
    grad_normed_two = matmul(grad_cq_low, cq_full, "rce,de->rcd")
    _, pull_two = jax.vjp(rms_norm, after_self, g_cross.astype(jnp.float32))
    part_two, grad_gain_cross = pull_two(grad_normed_two)
    grad_after_self = grad_after_cross + part_two
    self_in = (live_rows * grad_after_self).astype(jnp.bfloat16)
    grad_wout = matmul(attn_low, self_in, "rcd,rce->de")
    grad_self_attn = matmul(self_in, out_full, "rce,de->rcd").astype(jnp.bfloat16)

    def self_backward(carry, items):
        query_row, kv_row, seg_row, segk_row, lse_row, grad_row = items
        queries_h = query_row.reshape(local_len, HEADS, HEAD_DIM)
        grad_h = grad_row.reshape(local_len, HEADS, HEAD_DIM)
        key_row = kv_row[:, :D].reshape(LEN, HEADS, HEAD_DIM)
        value_row = kv_row[:, D:].reshape(LEN, HEADS, HEAD_DIM)
        scores = self_scores(queries_h, key_row, seg_row, segk_row)
        probs, grad_scores, centre = score_grads(scores, lse_row, value_row, grad_h)
        grad_query = matmul(grad_scores, key_row, "hqk,khd->qhd") * scale
        grad_key = matmul(grad_scores, queries_h, "hqk,qhd->khd") * scale
        grad_value = matmul(probs.astype(jnp.bfloat16), grad_h, "hqk,qhd->khd")
        kv_grads = jnp.concatenate([grad_key.reshape(LEN, D), grad_value.reshape(LEN, D)], axis=-1)
        return (
            carry + grad_scores.astype(jnp.float32),
            (grad_query.reshape(local_len, D), kv_grads, centre),
        )

    zero_block = jnp.zeros((HEADS, local_len, LEN), jnp.float32)
    score_total, (grad_q_rows, grad_kv_full, _) = lax.scan(
        self_backward, zero_block, (queries, key_all, seg_local, seg_all, lse_self, grad_self_attn)
    )
    grad_kv = lax.psum_scatter(
        grad_kv_full.astype(jnp.bfloat16), "seq", scatter_dimension=1, tiled=True
    )
    grad_bias = jnp.einsum(
        "hqk,qkb->bh", score_total, self_mask, precision=highest, preferred_element_type=jnp.float32
    )
    grad_qkv_low = jnp.concatenate([grad_q_rows.astype(jnp.bfloat16), grad_kv], axis=-1)
    grad_wqkv = matmul(hidden_one, grad_qkv_low, "rcd,rce->de")
    grad_normed_one = matmul(grad_qkv_low, qkv_full, "rce,de->rcd")
    _, pull_one = jax.vjp(rms_norm, dense, g_self.astype(jnp.float32))
    part_one, grad_gain_self = pull_one(grad_normed_one)
    grad_inputs = (grad_after_self + part_one).astype(jnp.bfloat16)
    (
        own_gself,
        own_qkv,
        own_wout,
        own_bias,
        own_gcross,
        own_cquery,
        own_ckv,
        own_cout,
        own_gff,
        own_gateup,
        own_down,
    ) = (
        lax.psum_scatter(
            grad_gain_self.astype(jnp.bfloat16), "dp", scatter_dimension=0, tiled=True
        ).astype(jnp.float32),
        lax.psum_scatter(
            grad_wqkv.astype(jnp.bfloat16), "dp", scatter_dimension=0, tiled=True
        ).astype(jnp.float32),
        lax.psum_scatter(
            grad_wout.astype(jnp.bfloat16), "dp", scatter_dimension=0, tiled=True
        ).astype(jnp.float32),
        lax.psum_scatter(
            grad_bias.astype(jnp.bfloat16), "dp", scatter_dimension=0, tiled=True
        ).astype(jnp.float32),
        lax.psum_scatter(
            grad_gain_cross.astype(jnp.bfloat16), "dp", scatter_dimension=0, tiled=True
        ).astype(jnp.float32),
        lax.psum_scatter(
            grad_cquery.astype(jnp.bfloat16), "dp", scatter_dimension=0, tiled=True
        ).astype(jnp.float32),
        lax.psum_scatter(
            grad_ckv.astype(jnp.bfloat16), "dp", scatter_dimension=0, tiled=True
        ).astype(jnp.float32),
        lax.psum_scatter(
            grad_cout.astype(jnp.bfloat16), "dp", scatter_dimension=0, tiled=True
        ).astype(jnp.float32),
        lax.psum_scatter(
            grad_gain_ff.astype(jnp.bfloat16), "dp", scatter_dimension=0, tiled=True
        ).astype(jnp.float32),
        lax.psum_scatter(
            grad_gate_up.astype(jnp.bfloat16), "dp", scatter_dimension=0, tiled=True
        ).astype(jnp.float32),
        lax.psum_scatter(
            grad_down.astype(jnp.bfloat16), "dp", scatter_dimension=0, tiled=True
        ).astype(jnp.float32),
    )
    summed = (
        lax.psum(own_gself.astype(jnp.bfloat16), "seq").astype(jnp.float32),
        lax.psum(own_qkv.astype(jnp.bfloat16), "seq").astype(jnp.float32),
        lax.psum(own_wout.astype(jnp.bfloat16), "seq").astype(jnp.float32),
        lax.psum(own_bias.astype(jnp.bfloat16), "seq").astype(jnp.float32),
        lax.psum(own_gcross.astype(jnp.bfloat16), "seq").astype(jnp.float32),
        lax.psum(own_cquery.astype(jnp.bfloat16), "seq").astype(jnp.float32),
        lax.psum(own_ckv.astype(jnp.bfloat16), "seq").astype(jnp.float32),
        lax.psum(own_cout.astype(jnp.bfloat16), "seq").astype(jnp.float32),
        lax.psum(own_gff.astype(jnp.bfloat16), "seq").astype(jnp.float32),
        lax.psum(own_gateup.astype(jnp.bfloat16), "seq").astype(jnp.float32),
        lax.psum(own_down.astype(jnp.bfloat16), "seq").astype(jnp.float32),
    )
    return (
        output,
        grad_inputs,
        grad_memory,
        summed[0],
        summed[1],
        summed[2],
        summed[3],
        summed[4],
        summed[5],
        summed[6],
        summed[7],
        summed[8],
        summed[9],
        summed[10],
    )


def solution(mesh):
    in_specs = (
        P("dp", "seq", None),
        P("dp", "seq", None),
        P("dp", "seq", None),
        P("dp", "seq"),
        P("dp"),
        P(),
        P("dp"),
        P("dp", None),
        P("dp", None),
        P("dp", None),
        P("dp"),
        P("dp", None),
        P("dp", None),
        P("dp", None),
        P("dp"),
        P("dp", None),
        P("dp", None),
    )
    out_specs = (
        P("dp", "seq", None),
        P("dp", "seq", None),
        P("dp", "seq", None),
        P("dp"),
        P("dp", None),
        P("dp", None),
        P("dp", None),
        P("dp"),
        P("dp", None),
        P("dp", None),
        P("dp", None),
        P("dp"),
        P("dp", None),
        P("dp", None),
    )
    return jax.shard_map(
        per_device, mesh=mesh, in_specs=in_specs, out_specs=out_specs, check_vma=False
    )
```

profile of v0, /device:TPU:0, one launch (start us, length us, event | category | flops | bytes accessed | tf_op | source)
XLA Modules:
  0.0 1443.8 jit_solution(10720891138837034868)
XLA Ops:
  8.8 41.4 %all-gather.16.cloned.1.call-done = bf16[768,1536]{1,0:T(8,128)(2,1)} async-done(((bf16[192,1536]{1,0:T(8,128)(2,1)}), bf16[768,1536]{1,0:T(8,128)(2,1)}) %all-gather.16.cloned.1.call-update) | async-done | bytes 2359312 | tf_op jit(solution)/shard_map/all_gather | solution.py:92
  55.6 9.2 all-reduce.10
  65.5 33.8 %all-gather.10.cloned.1.call-done = bf16[768,2304]{1,0:T(8,128)(2,1)} async-done(((bf16[192,2304]{1,0:T(8,128)(2,1)}), bf16[768,2304]{1,0:T(8,128)(2,1)}) %all-gather.10.cloned.1.call-update) | async-done | bytes 3538960 | tf_op jit(solution)/shard_map/all_gather | solution.py:87
  109.6 12.0 all_gather.55
  121.6 8.4 all_gather.56
  130.4 521.3 %gather_fusion = s32[131072]{0:T(1024)S(1)} fusion(s32[1024]{0:T(1024)S(1)} %copy-done.1, s32[131072]{0:T(1024)S(1)} %broadcast_clamp_fusion), kind=kCustom, calls=%fused_computation | custom fusion | bytes 1572864 | tf_op jit(solution)/shard_map/jit(_take)/gather | solution.py:44
  654.7 74.4 %copy.85 = pred[128,1024,32]{1,2,0:T(32,128)(4,1)S(1)} copy(pred[128,1024,32]{0,2,1:T(32,128)(4,1)S(1)} %iota_compare_fusion) | data formatting | bytes 8388608 | tf_op jit(solution)/shard_map/eq | solution.py:45
  731.2 6.3 copy.88
  738.4 8.7 copy.90
  747.1 8.8 copy.86
  756.6 19.4 %while.54 = (s32[]{:T(128)}, bf16[2,128,768]{1,2,0:T(8,128)(2,1)S(1)}, f32[2,12,128]{2,1,0:T(8,128)}, bf16[2,1024,1536]{1,2,0:T(8,128)(2,1)}, bf16[2,128]{1,0:T(...) while((s32[]{:T(128)}, ...), condition=%wide.region_4.5_spmd.clone, body=%wide.region_1.0_spmd.clone.sunk | while | flops 417593856 | bytes 61269428 | solution.py:135
  780.4 13.8 while.52
  796.4 6.8 fusion.24
  803.2 6.8 fusion.43
  814.4 28.9 %while.53 = (s32[]{:T(128)}, bf16[2,128,768]{1,2,0:T(8,128)(2,1)S(1)}, bf16[2,1024,1536]{1,2,0:T(8,128)(2,1)}, bf16[2,1024,1536]{1,2,0:T(8,128)(2,1)}, bf16[2,12...) while((s32[]{:T(128)}, ...), condition=%wide.region_14.15_spmd, body=%wide.region_12.14_spmd.sunk | while | flops 1033566720 | bytes 120662272 | solution.py:225
  843.3 16.6 %copy.120 = bf16[2,1024,1536]{2,0,1:T(2,128)(2,1)} copy(bf16[2,1024,1536]{1,2,0:T(8,128)(2,1)} %get-tuple-element.199) | data formatting | bytes 12582912
  859.9 7.0 copy.140
  872.8 59.3 %while.55 = (s32[]{:T(128)}, f32[12,128,1024]{2,1,0:T(8,128)}, bf16[2,128,768]{2,1,0:T(8,128)(2,1)}, bf16[2,1024,1536]{2,1,0:T(8,128)(2,1)}, bf16[2,128]{1,0:T(2...) while((s32[]{:T(128)}, f32[12,128,1024]{2,1,0:T(8,128)}, ...), condition=%wide.region_18.19_spmd.clone, body=%wide.region_16.18_spmd.clone.sunk | while | flops 1035926016 | bytes 178624096 | solution.py:261
  955.5 6.1 bitcast_convert_fusion
  961.7 43.0 %reduce-scatter.14.cloned.1.call-done = bf16[2,128,1536]{2,1,0:T(8,128)(2,1)} async-done(((bf16[2,1024,1536]{2,1,0:T(8,128)(2,1)}), bf16[2,128,1536]{2,1,0:T(8,128)(2,1)}) %reduce-scatter.14.cloned.1.call-update) | async-done | bytes 786448 | tf_op jit(solution)/shard_map/reduce_scatter | solution.py:264
  1009.1 34.2 %reduce-scatter.30.cloned.1.call-done = bf16[192,1536]{1,0:T(8,128)(2,1)} async-done(((bf16[768,1536]{1,0:T(8,128)(2,1)}), bf16[192,1536]{1,0:T(8,128)(2,1)}) %reduce-scatter.30.cloned.1.call-update) | async-done | bytes 589840
  1045.6 29.8 %reduce-scatter.22.cloned.1.call-done = bf16[192,768]{1,0:T(8,128)(2,1)} async-done(((bf16[768,768]{1,0:T(8,128)(2,1)}), bf16[192,768]{1,0:T(8,128)(2,1)}) %reduce-scatter.22.cloned.1.call-update) | async-done | bytes 294928 | tf_op jit(solution)/shard_map/reduce_scatter | solution.py:310
  1075.4 31.9 %reduce-scatter.20.cloned.1.call-done = bf16[192,768]{1,0:T(8,128)(2,1)} async-done(((bf16[768,768]{1,0:T(8,128)(2,1)}), bf16[192,768]{1,0:T(8,128)(2,1)}) %reduce-scatter.20.cloned.1.call-update) | async-done | bytes 294928 | tf_op jit(solution)/shard_map/reduce_scatter | solution.py:304
  1107.3 31.9 %reduce-scatter.18.cloned.1.call-done = bf16[192,768]{1,0:T(8,128)(2,1)} async-done(((bf16[768,768]{1,0:T(8,128)(2,1)}), bf16[192,768]{1,0:T(8,128)(2,1)}) %reduce-scatter.18.cloned.1.call-update) | async-done | bytes 294928 | tf_op jit(solution)/shard_map/reduce_scatter | solution.py:295
  1139.2 47.4 %reduce-scatter.26.cloned.1.call-done = bf16[512,768]{1,0:T(8,128)(2,1)} async-done(((bf16[2048,768]{1,0:T(8,128)(2,1)}), bf16[512,768]{1,0:T(8,128)(2,1)}) %reduce-scatter.26.cloned.1.call-update) | async-done | bytes 786448 | tf_op jit(solution)/shard_map/reduce_scatter | solution.py:319
  1186.6 73.1 %reduce-scatter.24.cloned.1.call-done = bf16[192,4096]{1,0:T(8,128)(2,1)} async-done(((bf16[768,4096]{1,0:T(8,128)(2,1)}), bf16[192,4096]{1,0:T(8,128)(2,1)}) %reduce-scatter.24.cloned.1.call-update) | async-done | bytes 1572880 | tf_op jit(solution)/shard_map/reduce_scatter | solution.py:316
  1259.6 50.2 %reduce-scatter.16.cloned.1.call-done = bf16[192,2304]{1,0:T(8,128)(2,1)} async-done(((bf16[768,2304]{1,0:T(8,128)(2,1)}), bf16[192,2304]{1,0:T(8,128)(2,1)}) %reduce-scatter.16.cloned.1.call-update) | async-done | bytes 884752 | tf_op jit(solution)/shard_map/reduce_scatter | solution.py:292
  1311.1 9.1 copy.105
  1323.9 11.3 fusion.64
  1336.6 15.0 %all-reduce.9 = (bf16[768]{0:T(1024)(128)(2,1)S(1)}, bf16[32,12]{1,0:T(8,128)(2,1)S(1)}, bf16[768]{0:T(1024)(128)(2,1)S(1)}, bf16[768]{0:T(1024)(128)(2,1)S(1)}) all-reduce(bf16[768]{0:T(1024)(128)(2,1)S(1)} %get-tuple-element.409, bf16[32,12]{1,0:T(8,128)(2,1)S(1)} %fusion.64, ...), channel_id=4, replica_groups=mesh['dp'=4,'seq'=8] {'dp'}, use_global_device_ids=true, to_apply=%region_23.24.clone | all-reduce | flops 2688 | bytes 10752
  1351.8 14.6 %all-reduce.7 = (bf16[192]{0:T(256)(128)(2,1)S(1)}, bf16[8,12]{1,0:T(8,128)(2,1)S(1)}, bf16[192]{0:T(256)(128)(2,1)S(1)}, bf16[192]{0:T(256)(128)(2,1)S(1)}) all-reduce(bf16[192]{0:T(256)(128)(2,1)S(1)} %dynamic-slice.4, bf16[8,12]{1,0:T(8,128)(2,1)S(1)} %constant_dynamic-slice_fusion.8, ...), channel_id=1, replica_groups=mesh['dp'=4,'seq'=8] {'seq'}, use_global_device_ids=true, to_apply=%region_24.25 | all-reduce | flops 672 | bytes 2688 | tf_op jit(solution)/shard_map/psum | solution.py:324
  1372.9 52.5 %all-reduce.13.cloned.1.call-done = (bf16[192,1536]{0,1:T(8,128)(2,1)}, bf16[192,2304]{1,0:T(8,128)(2,1)}, bf16[192,768]{1,0:T(8,128)(2,1)}, bf16[192,768]{1,0:T...) async-done(((bf16[192,1536]{0,1:T(8,128)(2,1)}, bf16[192,2304]{1,0:T(8,128)(2,1)}, bf16[192,768]{1,0:T(8,128)(2,1)}, ...) | async-done | bytes 4718608 | tf_op jit(solution)/shard_map/psum | solution.py:330
  (450 shorter events, 214.3 us)
Async XLA Ops:
  7.2 46.4 %copy-start.72 = (u32[32]{0:T(128)S(1)}, u32[32]{0:T(128)}, u32[]{:S(2)}) copy-start(u32[32]{0:T(128)} %constant.142) | copy-start | bytes 388
  7.2 47.6 %copy-start.78 = (bf16[192]{0:T(256)(128)(2,1)S(1)}, bf16[192]{0:T(256)(128)(2,1)}, u32[]{:S(2)}) copy-start(bf16[192]{0:T(256)(128)(2,1)} %param.35) | copy-start | bytes 1156
  7.2 47.9 %copy-start.79 = (bf16[192]{0:T(256)(128)(2,1)S(1)}, bf16[192]{0:T(256)(128)(2,1)}, u32[]{:S(2)}) copy-start(bf16[192]{0:T(256)(128)(2,1)} %param.31) | copy-start | bytes 1156
  7.2 48.1 %copy-start.80 = (bf16[192]{0:T(256)(128)(2,1)S(1)}, bf16[192]{0:T(256)(128)(2,1)}, u32[]{:S(2)}) copy-start(bf16[192]{0:T(256)(128)(2,1)} %param.39) | copy-start | bytes 1156
  7.2 57.5 %copy-start.13 = (bf16[2,128,768]{2,1,0:T(8,128)(2,1)S(1)}, bf16[2,128,768]{2,1,0:T(8,128)(2,1)}, u32[]{:S(2)}) copy-start(bf16[2,128,768]{2,1,0:T(8,128)(2,1)} %param.25) | copy-start | bytes 1179652
  7.2 42.9 %all-gather.16.cloned.1.call-start = ((), (), s32[]{:S(2)}) async-start(), calls=%async_computation.12 | async-start | bytes 2949120 | tf_op jit(solution)/shard_map/all_gather | solution.py:92
  8.0 91.3 %all-gather.10.cloned.1.call-start = ((), (), s32[]{:S(2)}) async-start(), calls=%async_computation.9 | async-start | bytes 4423680 | tf_op jit(solution)/shard_map/all_gather | solution.py:87
  8.7 729.7 %all-gather.18.cloned.1.call-start = ((), (), s32[]{:S(2)}) async-start(), calls=%async_computation.13 | async-start | bytes 7077888 | tf_op jit(solution)/shard_map/all_gather | solution.py:143
  53.5 693.6 %all-gather.12.cloned.1.call-start = ((), (), s32[]{:S(2)}) async-start(), calls=%async_computation.10 | async-start | bytes 7077888 | tf_op jit(solution)/shard_map/all_gather | solution.py:110
  104.4 671.6 %all-gather.14.cloned.1.call-start = ((), (), s32[]{:S(2)}) async-start(), calls=%async_computation.11 | async-start | bytes 1474560 | tf_op jit(solution)/shard_map/all_gather | solution.py:88
  105.0 673.1 %all-gather.20.cloned.1.call-start = ((), (), s32[]{:S(2)}) async-start(), calls=%async_computation.14 | async-start | bytes 1474560 | tf_op jit(solution)/shard_map/all_gather | solution.py:91
  105.6 688.8 %all-gather.22.cloned.1.call-start = ((), (), s32[]{:S(2)}) async-start(), calls=%async_computation.15 | async-start | bytes 1474560 | tf_op jit(solution)/shard_map/all_gather | solution.py:93
  106.3 690.0 %all-gather.24.cloned.1.call-start = ((), (), s32[]{:S(2)}) async-start(), calls=%async_computation.16 | async-start | bytes 7864320 | tf_op jit(solution)/shard_map/all_gather | solution.py:95
  107.1 696.2 %all-gather.26.cloned.1.call-start = ((), (), s32[]{:S(2)}) async-start(), calls=%async_computation.17 | async-start | bytes 3932160 | tf_op jit(solution)/shard_map/all_gather | solution.py:96
  107.8 826.3 %reduce-scatter.28.cloned.1.call-start = ((), (), s32[]{:S(2)}) async-start(), calls=%async_computation.25 | async-start | bytes 7077888
  130.4 521.4 %copy-start.53 = (s32[128]{0:T(128)S(1)}, s32[128]{0:T(128)}, u32[]{:S(2)}) copy-start(s32[128]{0:T(128)} %copy-done.52) | copy-start | bytes 1540
  652.3 76.8 %copy-start.18 = (s32[128,1024]{0,1:T(8,128)}, s32[128,1024]{0,1:T(8,128)S(1)}, u32[]{:S(2)}) copy-start(s32[128,1024]{0,1:T(8,128)S(1)} %copy.84) | copy-start | bytes 1572868
  654.7 74.5 %copy-start.57 = (bf16[32,12]{1,0:T(8,128)(2,1)S(1)}, bf16[32,12]{1,0:T(8,128)(2,1)}, u32[]{:S(2)}) copy-start(bf16[32,12]{1,0:T(8,128)(2,1)} %all_gather.56) | copy-start | bytes 2308
  778.0 92.3 %copy-start.5 = (f32[2,128,768]{2,1,0:T(8,128)}, f32[2,128,768]{2,1,0:T(8,128)S(1)}, u32[]{:S(2)}) copy-start(f32[2,128,768]{2,1,0:T(8,128)S(1)} %get-tuple-element.519) | copy-start | bytes 2359300
  813.8 56.5 %copy-start.11 = (f32[2,128,768]{2,1,0:T(8,128)}, f32[2,128,768]{2,1,0:T(8,128)S(1)}, u32[]{:S(2)}) copy-start(f32[2,128,768]{2,1,0:T(8,128)S(1)} %convert_add_fusion.1) | copy-start | bytes 2359300
  867.0 137.7 %reduce-scatter.14.cloned.1.call-start = ((), (), s32[]{:S(2)}) async-start(), calls=%async_computation.18 | async-start | bytes 7077888 | tf_op jit(solution)/shard_map/reduce_scatter | solution.py:264
  932.1 111.2 %reduce-scatter.30.cloned.1.call-start = ((), (), s32[]{:S(2)}) async-start(), calls=%async_computation.26 | async-start | bytes 2949120
  944.2 131.2 %reduce-scatter.22.cloned.1.call-start = ((), (), s32[]{:S(2)}) async-start(), calls=%async_computation.22 | async-start | bytes 1474560 | tf_op jit(solution)/shard_map/reduce_scatter | solution.py:310
  946.0 161.2 %reduce-scatter.20.cloned.1.call-start = ((), (), s32[]{:S(2)}) async-start(), calls=%async_computation.21 | async-start | bytes 1474560 | tf_op jit(solution)/shard_map/reduce_scatter | solution.py:304
  948.9 190.3 %reduce-scatter.18.cloned.1.call-start = ((), (), s32[]{:S(2)}) async-start(), calls=%async_computation.20 | async-start | bytes 1474560 | tf_op jit(solution)/shard_map/reduce_scatter | solution.py:295
  951.5 235.1 %reduce-scatter.26.cloned.1.call-start = ((), (), s32[]{:S(2)}) async-start(), calls=%async_computation.24 | async-start | bytes 3932160 | tf_op jit(solution)/shard_map/reduce_scatter | solution.py:319
  954.4 305.3 %reduce-scatter.24.cloned.1.call-start = ((), (), s32[]{:S(2)}) async-start(), calls=%async_computation.23 | async-start | bytes 7864320 | tf_op jit(solution)/shard_map/reduce_scatter | solution.py:316
  961.6 43.0 %copy-start.15 = (bf16[2,128,768]{2,1,0:T(8,128)(2,1)S(1)}, bf16[2,128,768]{2,1,0:T(8,128)(2,1)}, u32[]{:S(2)}) copy-start(bf16[2,128,768]{2,1,0:T(8,128)(2,1)} %param.25) | copy-start | bytes 1179652
  961.6 43.0 %copy-start.48 = (f32[768]{0:T(1024)S(1)}, f32[768]{0:T(1024)}, u32[]{:S(2)}) copy-start(f32[768]{0:T(1024)} %copy-done.47) | copy-start | bytes 9220
  961.6 43.0 %copy-start.64 = (f32[2,128]{1,0:T(2,128)S(1)}, f32[2,128]{1,0:T(2,128)}, u32[]{:S(2)}) copy-start(f32[2,128]{1,0:T(2,128)} %copy-done.63) | copy-start | bytes 3076
  961.6 348.2 %reduce-scatter.16.cloned.1.call-start = ((), (), s32[]{:S(2)}) async-start(), calls=%async_computation.19 | async-start | bytes 4423680 | tf_op jit(solution)/shard_map/reduce_scatter | solution.py:292
  1009.0 416.5 %all-reduce.13.cloned.1.call-start = ((), (), s32[]{:S(2)}) async-start(), calls=%async_computation.27 | async-start | bytes 9830400 | tf_op jit(solution)/shard_map/psum | solution.py:330
  (92 other events, 671.8 us)
Sparse Core Ops, SparseCore 0:
  9.9 40.1 all-gather.15
  52.0 47.2 all-gather.9
  101.4 64.7 all-gather.17
  168.3 63.3 all-gather.11
  233.4 26.4 all-gather.13
  261.5 27.7 all-gather.19
  291.1 27.7 all-gather.21
  320.8 70.1 all-gather.23
  392.8 43.9 all-gather.25
  867.1 67.0 reduce-scatter.27
  936.4 68.1 reduce-scatter.13
  1007.5 35.7 reduce-scatter.29
  1046.8 28.5 reduce-scatter.21
  1078.7 28.5 reduce-scatter.19
  1110.6 28.5 reduce-scatter.17
  1142.6 43.9 reduce-scatter.25
  1189.4 70.1 reduce-scatter.23
  1262.6 47.2 reduce-scatter.15
  1312.8 112.6 all-reduce.12
where the time goes:
time: 1450 us; the launch traced here: 1440 us
  local copies, waits for them, and re-layouts  733 us (51%)
  waiting for transfers between devices  476 us (33%)
  matrix products  120 us (8%)
  blocking collectives  59.1 us (4%)
  other arithmetic  36.5 us (3%)
  between operations  17.1 us (1%)
    gather x2, local copies, waits for them, and re-layouts, bucket_mask(): bucket_of = jnp.take(buckets, jnp.clip(offsets, 0, LEN - 1), axis=0)  521 us
    dot_general x49, matrix products, matmul(): return jnp.einsum(form, left, right, preferred_element_type=jnp.float32)  106 us
    eq x1, local copies, waits for them, and re-layouts, bucket_mask(): bucket_of[..., None] == jnp.arange(BUCKETS, dtype=jnp.int32)  74.4 us
    reduce_scatter x1, waiting for transfers between devices, per_device(): lax.psum_scatter(grad_gate_up.astype(jnp.bfloat16), 'dp', scatter_dimensi...  73.1 us
    unnamed x174, local copies, waits for them, and re-layouts  58.8 us
    psum x1, waiting for transfers between devices, per_device(): lax.psum(own_ckv.astype(jnp.bfloat16), 'seq').astype(jnp.float32)  52.5 us
    reduce_scatter x1, waiting for transfers between devices, per_device(): lax.psum_scatter(grad_wqkv.astype(jnp.bfloat16), 'dp', scatter_dimension=...  50.2 us
    reduce_scatter x1, waiting for transfers between devices, per_device(): lax.psum_scatter(grad_down.astype(jnp.bfloat16), 'dp', scatter_dimension=...  47.4 us
  transfers between devices with their start and end apart: 19, of which 12 were waited for; matrix products, arithmetic and copies ran while one was open for 56% of the time, Pallas kernels for 0%

commit v1 on v0

--- a/solution.py
+++ b/solution.py
@@ -40,15 +40,26 @@
     return (probs, grad_scores, centre[..., 0])
 
 
-def bucket_mask(buckets, offsets):
-    bucket_of = jnp.take(buckets, jnp.clip(offsets, 0, LEN - 1), axis=0)
-    return (bucket_of[..., None] == jnp.arange(BUCKETS, dtype=jnp.int32)).astype(jnp.float32)
-
-
-def bias_from(table, mask):
-    return jnp.einsum(
-        "qkb,bh->hqk", mask, table, precision=highest, preferred_element_type=jnp.float32
-    )
+def one_hot_of(buckets):
+    return (buckets[:, None] == jnp.arange(BUCKETS, dtype=jnp.int32)).astype(jnp.float32)
+
+
+def skewed(by_dist, start, rows):
+    table = jnp.concatenate([jnp.zeros((LEN - 1, HEADS), by_dist.dtype), by_dist], axis=0)
+    window = lax.dynamic_slice_in_dim(table, start, rows + LEN - 1, axis=0)
+    line = jnp.pad(window[::-1].T, ((0, 0), (0, 1)))
+    width = rows + LEN
+    flat = jnp.broadcast_to(line[:, None, :], (HEADS, rows, width)).reshape(HEADS, rows * width)
+    return flat[:, : rows * (width - 1)].reshape(HEADS, rows, width - 1)[:, :, rows - 1 :]
+
+
+def unskewed(block, start, rows):
+    width = rows + LEN
+    wide = jnp.pad(block, ((0, 0), (0, 0), (rows - 1, 0))).reshape(HEADS, rows * (width - 1))
+    line = jnp.sum(jnp.pad(wide, ((0, 0), (0, rows))).reshape(HEADS, rows, width), axis=1)
+    window = line[:, : width - 1][:, ::-1].T
+    table = jnp.zeros((2 * LEN - 1, HEADS), block.dtype)
+    return lax.dynamic_update_slice_in_dim(table, window, start, axis=0)[LEN - 1 :]
 
 
 def per_device(
@@ -113,8 +124,15 @@
     positions = seq_index * local_len + jnp.arange(local_len, dtype=jnp.int32)
     offsets = positions[:, None] - jnp.arange(LEN, dtype=jnp.int32)[None, :]
     causal = offsets >= 0
-    self_mask = bucket_mask(buckets, offsets)
-    bias_block = bias_from(bias_full.astype(jnp.float32), self_mask)
+    bucket_hot = one_hot_of(buckets)
+    by_dist = jnp.einsum(
+        "lb,bh->lh",
+        bucket_hot,
+        bias_full.astype(jnp.float32),
+        precision=highest,
+        preferred_element_type=jnp.float32,
+    )
+    bias_block = skewed(by_dist, seq_index * local_len, local_len)
 
     def self_scores(queries_h, key_row, seg_row, segk_row):
         raw = matmul(queries_h, key_row, "qhd,khd->hqk") * scale + bias_block
@@ -265,7 +283,11 @@
         grad_kv_full.astype(jnp.bfloat16), "seq", scatter_dimension=1, tiled=True
     )
     grad_bias = jnp.einsum(
-        "hqk,qkb->bh", score_total, self_mask, precision=highest, preferred_element_type=jnp.float32
+        "lh,lb->bh",
+        unskewed(score_total, seq_index * local_len, local_len),
+        bucket_hot,
+        precision=highest,
+        preferred_element_type=jnp.float32,
     )
     grad_qkv_low = jnp.concatenate([grad_q_rows.astype(jnp.bfloat16), grad_kv], axis=-1)
     grad_wqkv = matmul(hidden_one, grad_qkv_low, "rcd,rce->de")

time: 1450 us -> 1120 us (0.77)
  local copies, waits for them, and re-layouts: 733 us -> 196 us
  waiting for transfers between devices: 476 us -> 670 us
    gather x2 -> x0, local copies, waits for them, and re-layouts: 521 us -> none  [bucket_mask(): bucket_of = jnp.take(buckets, jnp.clip(offsets, 0, LEN - 1), axis=0)]
    eq x1 -> x0, local copies, waits for them, and re-layouts: 74.4 us -> none  [bucket_mask(): bucket_of[..., None] == jnp.arange(BUCKETS, dtype=jnp.int32)]
    all_gather x1, waiting for transfers between devices: 0.02 us -> 70.1 us  [per_device(): lax.all_gather(w_gate_up, 'dp', axis=0, tiled=True)]
    all_gather x1, waiting for transfers between devices: 0.01 us -> 56.7 us  [per_device(): lax.all_gather(key_value, 'seq', axis=1, tiled=True)]
    all_gather x1, waiting for transfers between devices: 0.01 us -> 39.2 us  [per_device(): lax.all_gather(w_down, 'dp', axis=0, tiled=True)]
    unnamed x21, waiting for transfers between devices: 40.9 us -> 8.87 us
    reshape x0 -> x2, local copies, waits for them, and re-layouts: none -> 29.8 us  [the longest x1 16 us: skewed(): flat[:, :rows * (width - 1)].reshape(HEADS, rows, width - 1)]
    all_gather x1, waiting for transfers between devices: 0.02 us -> 25.6 us  [per_device(): lax.all_gather(c_query, 'dp', axis=0, tiled=True)]
  transfers between devices with their start and end apart: 19 -> 19, of which waited for: 12 -> 17; matrix products, arithmetic and copies ran while one was open for 56% -> 23% of each run, Pallas kernels for 0% -> 0%
where the time goes in v1:
time: 1120 us; the launch traced here: 1110 us
  waiting for transfers between devices  670 us (60%)
  local copies, waits for them, and re-layouts  196 us (18%)
  matrix products  126 us (11%)
  blocking collectives  58.7 us (5%)
  other arithmetic  40 us (4%)
  between operations  17.1 us (2%)
    dot_general x49, matrix products, matmul(): return jnp.einsum(form, left, right, preferred_element_type=jnp.float32)  125 us
    reduce_scatter x1, waiting for transfers between devices, per_device(): lax.psum_scatter(grad_gate_up.astype(jnp.bfloat16), 'dp', scatter_dimensi...  73.1 us
    psum x1, waiting for transfers between devices, per_device(): lax.psum(own_ckv.astype(jnp.bfloat16), 'seq').astype(jnp.float32)  72.5 us
    all_gather x1, waiting for transfers between devices, per_device(): lax.all_gather(w_gate_up, 'dp', axis=0, tiled=True)  70.1 us
    unnamed x187, local copies, waits for them, and re-layouts  62.5 us
    all_gather x1, waiting for transfers between devices, per_device(): lax.all_gather(key_value, 'seq', axis=1, tiled=True)  56.7 us
    reduce_scatter x1, waiting for transfers between devices, per_device(): lax.psum_scatter(grad_wqkv.astype(jnp.bfloat16), 'dp', scatter_dimension=...  50.2 us
    reduce_scatter x1, waiting for transfers between devices, per_device(): lax.psum_scatter(grad_down.astype(jnp.bfloat16), 'dp', scatter_dimension=...  47.4 us
  transfers between devices with their start and end apart: 19, of which 17 were waited for; matrix products, arithmetic and copies ran while one was open for 23% of the time, Pallas kernels for 0%

profile of v1, /device:TPU:0, one launch (start us, length us, event | category | flops | bytes accessed | tf_op | source)
XLA Modules:
  0.0 1110.8 jit_solution(6622182637633407842)
XLA Ops:
  8.8 41.4 %all-gather.16.cloned.1.call-done = bf16[768,1536]{1,0:T(8,128)(2,1)} async-done(((bf16[192,1536]{1,0:T(8,128)(2,1)}), bf16[768,1536]{1,0:T(8,128)(2,1)}) %all-gather.16.cloned.1.call-update) | async-done | bytes 2359312 | tf_op jit(solution)/shard_map/all_gather | solution.py:103
  55.5 9.2 all-reduce.14
  65.5 33.8 %all-gather.10.cloned.1.call-done = bf16[768,2304]{1,0:T(8,128)(2,1)} async-done(((bf16[192,2304]{1,0:T(8,128)(2,1)}), bf16[768,2304]{1,0:T(8,128)(2,1)}) %all-gather.10.cloned.1.call-update) | async-done | bytes 3538960 | tf_op jit(solution)/shard_map/all_gather | solution.py:98
  108.4 11.9 %all_gather.55 = bf16[2,1024]{1,0:T(2,128)(2,1)S(1)} all-gather(bf16[2,128]{1,0:T(2,128)(2,1)} %convert_element_type.213), channel_id=1, replica_groups=mesh['dp'=4,'seq'=8] {'seq'}, dimensions={1}, use_global_device_ids=true | all-gather | bytes 4608 | tf_op jit(solution)/shard_map/all_gather | solution.py:122
  120.3 8.0 all_gather.56
  140.4 16.0 %reshape.296 = f32[12,128,1151]{2,1,0:T(8,128)} reshape(f32[12,147328]{1,0:T(8,128)} %slice.70) | data formatting | bytes 14143488 | tf_op jit(solution)/shard_map/reshape | solution.py:53
  156.4 7.4 slice.71
  166.2 8.7 copy.56
  174.9 56.7 %all-gather.12.cloned.1.call-done = bf16[2,1024,1536]{2,1,0:T(8,128)(2,1)} async-done(((bf16[2,128,1536]{2,1,0:T(8,128)(2,1)}), bf16[2,1024,1536]{2,1,0:T(8,128)(2,1)}) %all-gather.12.cloned.1.call-update) | async-done | bytes 6291472 | tf_op jit(solution)/shard_map/all_gather | solution.py:121
  231.7 8.6 copy.53
  240.9 20.7 %while.54 = (s32[]{:T(128)}, bf16[2,128,768]{1,2,0:T(8,128)(2,1)S(1)}, f32[2,12,128]{2,1,0:T(8,128)}, bf16[2,1024,1536]{1,2,0:T(8,128)(2,1)}, bf16[2,128]{1,0:T(...) while((s32[]{:T(128)}, ...), condition=%wide.region_4.5_spmd.clone, body=%wide.region_1.4_spmd.clone.sunk | while | flops 417593856 | bytes 67560856 | solution.py:153
  263.7 25.6 %all-gather.20.cloned.1.call-done = bf16[768,768]{1,0:T(8,128)(2,1)} async-done(((bf16[192,768]{1,0:T(8,128)(2,1)}), bf16[768,768]{1,0:T(8,128)(2,1)}) %all-gather.20.cloned.1.call-update) | async-done | bytes 1179664 | tf_op jit(solution)/shard_map/all_gather | solution.py:102
  291.4 13.9 %while.52 = (s32[]{:T(128)}, bf16[2,128,768]{1,2,0:T(8,128)(2,1)S(1)}, f32[2,12,128]{2,1,0:T(8,128)S(1)}, bf16[2,1024,1536]{1,2,0:T(8,128)(2,1)}, bf16[2,128,768]{1,2,0:T(8,128)(2,1)S(1)}, /*index=5*/s32[]{:T(128)}) while((s32[]{:T(128)}, bf16[2,128,768]{1,2,0:T(8,128)(2,1)S(1)}, f32[2,12,128]{2,1,0:T(8,128)S(1)}, ...), condition=%wide.region_9.10_spmd, body=%wide.region_6.9_spmd.sunk | while | flops 416807424 | bytes 35838044 | solution.py:174
  305.4 13.6 %all-gather.22.cloned.1.call-done = bf16[768,768]{1,0:T(8,128)(2,1)} async-done(((bf16[192,768]{1,0:T(8,128)(2,1)}), bf16[768,768]{1,0:T(8,128)(2,1)}) %all-gather.22.cloned.1.call-update) | async-done | bytes 1179664 | tf_op jit(solution)/shard_map/all_gather | solution.py:104
  320.8 70.1 %all-gather.24.cloned.1.call-done = bf16[768,4096]{1,0:T(8,128)(2,1)} async-done(((bf16[192,4096]{1,0:T(8,128)(2,1)}), bf16[768,4096]{1,0:T(8,128)(2,1)}) %all-gather.24.cloned.1.call-update) | async-done | bytes 6291472 | tf_op jit(solution)/shard_map/all_gather | solution.py:106
  397.6 39.2 %all-gather.26.cloned.1.call-done = bf16[2048,768]{1,0:T(8,128)(2,1)} async-done(((bf16[512,768]{1,0:T(8,128)(2,1)}), bf16[2048,768]{1,0:T(8,128)(2,1)}) %all-gather.26.cloned.1.call-update) | async-done | bytes 3145744 | tf_op jit(solution)/shard_map/all_gather | solution.py:107
  436.8 7.0 fusion.43
  449.7 47.3 %while.53 = (s32[]{:T(128)}, bf16[2,128,768]{1,2,0:T(8,128)(2,1)}, bf16[2,1024,1536]{1,2,0:T(8,128)(2,1)}, bf16[2,1024,1536]{1,2,0:T(8,128)(2,1)}, bf16[2,128,76...) while((s32[]{:T(128)}, bf16[2,128,768]{1,2,0:T(8,128)(2,1)}, ...), condition=%wide.region_14.15_spmd, body=%wide.region_12.14_spmd.sunk | while | flops 1033566720 | bytes 149711344 | solution.py:243
  497.1 16.5 %copy.84 = bf16[2,1024,1536]{2,0,1:T(2,128)(2,1)} copy(bf16[2,1024,1536]{1,2,0:T(8,128)(2,1)} %get-tuple-element.199) | data formatting | bytes 12582912
  526.4 75.4 %while.55 = (s32[]{:T(128)}, f32[12,128,1024]{2,1,0:T(8,128)}, bf16[2,128,768]{2,1,0:T(8,128)(2,1)}, bf16[2,1024,1536]{2,1,0:T(8,128)(2,1)}, bf16[2,128]{1,0:T(2...) while((s32[]{:T(128)}, f32[12,128,1024]{2,1,0:T(8,128)}, ...), condition=%wide.region_18.19_spmd.clone, body=%wide.region_16.18_spmd.clone.sunk | while | flops 1035926016 | bytes 161322656 | solution.py:279
  628.9 43.4 %reduce-scatter.14.cloned.1.call-done = bf16[2,128,1536]{2,1,0:T(8,128)(2,1)} async-done(((bf16[2,1024,1536]{2,1,0:T(8,128)(2,1)}), bf16[2,128,1536]{2,1,0:T(8,128)(2,1)}) %reduce-scatter.14.cloned.1.call-update) | async-done | bytes 786448 | tf_op jit(solution)/shard_map/reduce_scatter | solution.py:282
  677.7 8.0 pad.14
  685.6 13.8 %reshape.297 = f32[12,147328]{1,0:T(8,128)} reshape(f32[12,128,1151]{2,1,0:T(8,128)} %pad.14) | data formatting | bytes 14143488 | tf_op jit(solution)/shard_map/reshape | solution.py:58
  713.2 29.9 %reduce-scatter.18.cloned.1.call-done = bf16[192,768]{1,0:T(8,128)(2,1)} async-done(((bf16[768,768]{1,0:T(8,128)(2,1)}), bf16[192,768]{1,0:T(8,128)(2,1)}) %reduce-scatter.18.cloned.1.call-update) | async-done | bytes 294928 | tf_op jit(solution)/shard_map/reduce_scatter | solution.py:317
  743.1 31.9 %reduce-scatter.20.cloned.1.call-done = bf16[192,768]{1,0:T(8,128)(2,1)} async-done(((bf16[768,768]{1,0:T(8,128)(2,1)}), bf16[192,768]{1,0:T(8,128)(2,1)}) %reduce-scatter.20.cloned.1.call-update) | async-done | bytes 294928 | tf_op jit(solution)/shard_map/reduce_scatter | solution.py:326
  775.0 31.9 %reduce-scatter.22.cloned.1.call-done = bf16[192,768]{1,0:T(8,128)(2,1)} async-done(((bf16[768,768]{1,0:T(8,128)(2,1)}), bf16[192,768]{1,0:T(8,128)(2,1)}) %reduce-scatter.22.cloned.1.call-update) | async-done | bytes 294928 | tf_op jit(solution)/shard_map/reduce_scatter | solution.py:332
  806.9 47.4 %reduce-scatter.26.cloned.1.call-done = bf16[512,768]{1,0:T(8,128)(2,1)} async-done(((bf16[2048,768]{1,0:T(8,128)(2,1)}), bf16[512,768]{1,0:T(8,128)(2,1)}) %reduce-scatter.26.cloned.1.call-update) | async-done | bytes 786448 | tf_op jit(solution)/shard_map/reduce_scatter | solution.py:341
  854.3 73.1 %reduce-scatter.24.cloned.1.call-done = bf16[192,4096]{1,0:T(8,128)(2,1)} async-done(((bf16[768,4096]{1,0:T(8,128)(2,1)}), bf16[192,4096]{1,0:T(8,128)(2,1)}) %reduce-scatter.24.cloned.1.call-update) | async-done | bytes 1572880 | tf_op jit(solution)/shard_map/reduce_scatter | solution.py:338
  927.3 50.2 %reduce-scatter.16.cloned.1.call-done = bf16[192,2304]{1,0:T(8,128)(2,1)} async-done(((bf16[768,2304]{1,0:T(8,128)(2,1)}), bf16[192,2304]{1,0:T(8,128)(2,1)}) %reduce-scatter.16.cloned.1.call-update) | async-done | bytes 884752 | tf_op jit(solution)/shard_map/reduce_scatter | solution.py:314
  984.1 15.1 %all-reduce.13 = (bf16[768]{0:T(1024)(128)(2,1)S(1)}, bf16[32,12]{1,0:T(8,128)(2,1)S(1)}, bf16[768]{0:T(1024)(128)(2,1)S(1)}, bf16[768]{0:T(1024)(128)(2,1)S(1)}) all-reduce(bf16[768]{0:T(1024)(128)(2,1)S(1)} %get-tuple-element.362, bf16[32,12]{1,0:T(8,128)(2,1)S(1)} %convolution_convert_fusion.5, ...), channel_id=4, replica_groups=mesh['dp'=4,'seq'=8] {'dp'}, use_global_device_ids=true, to_apply=%region_23.24.clone | all-reduce | flops 2688 | bytes 10752
  999.4 14.6 %all-reduce.11 = (bf16[192]{0:T(256)(128)(2,1)S(1)}, bf16[8,12]{1,0:T(8,128)(2,1)S(1)}, bf16[192]{0:T(256)(128)(2,1)S(1)}, bf16[192]{0:T(256)(128)(2,1)S(1)}) all-reduce(bf16[192]{0:T(256)(128)(2,1)S(1)} %dynamic-slice.4, bf16[8,12]{1,0:T(8,128)(2,1)S(1)} %constant_dynamic-slice_fusion.8, ...), channel_id=1, replica_groups=mesh['dp'=4,'seq'=8] {'seq'}, use_global_device_ids=true, to_apply=%region_24.25 | all-reduce | flops 672 | bytes 2688 | tf_op jit(solution)/shard_map/psum | solution.py:346
  1020.6 72.5 %all-reduce.17.cloned.1.call-done = (bf16[192,1536]{0,1:T(8,128)(2,1)}, bf16[192,2304]{1,0:T(8,128)(2,1)}, bf16[192,768]{1,0:T(8,128)(2,1)}, bf16[192,768]{1,0:T...) async-done(((bf16[192,1536]{0,1:T(8,128)(2,1)}, bf16[192,2304]{1,0:T(8,128)(2,1)}, bf16[192,768]{1,0:T(8,128)(2,1)}, ...) | async-done | bytes 4718608 | tf_op jit(solution)/shard_map/psum | solution.py:352
  (508 shorter events, 287.3 us)
Async XLA Ops:
  7.2 47.8 %copy-start.94 = (bf16[192]{0:T(256)(128)(2,1)S(1)}, bf16[192]{0:T(256)(128)(2,1)}, u32[]{:S(2)}) copy-start(bf16[192]{0:T(256)(128)(2,1)} %param.35) | copy-start | bytes 1156
  7.2 48.1 %copy-start.95 = (bf16[192]{0:T(256)(128)(2,1)S(1)}, bf16[192]{0:T(256)(128)(2,1)}, u32[]{:S(2)}) copy-start(bf16[192]{0:T(256)(128)(2,1)} %param.39) | copy-start | bytes 1156
  7.2 57.5 %copy-start.24 = (bf16[2,128,768]{2,1,0:T(8,128)(2,1)S(1)}, bf16[2,128,768]{2,1,0:T(8,128)(2,1)}, u32[]{:S(2)}) copy-start(bf16[2,128,768]{2,1,0:T(8,128)(2,1)} %param.25) | copy-start | bytes 1179652
  7.3 42.9 %all-gather.16.cloned.1.call-start = ((), (), s32[]{:S(2)}) async-start(), calls=%async_computation.12 | async-start | bytes 2949120 | tf_op jit(solution)/shard_map/all_gather | solution.py:103
  8.0 91.3 %all-gather.10.cloned.1.call-start = ((), (), s32[]{:S(2)}) async-start(), calls=%async_computation.9 | async-start | bytes 4423680 | tf_op jit(solution)/shard_map/all_gather | solution.py:98
  8.7 157.5 %all-gather.18.cloned.1.call-start = ((), (), s32[]{:S(2)}) async-start(), calls=%async_computation.13 | async-start | bytes 7077888 | tf_op jit(solution)/shard_map/all_gather | solution.py:161
  53.5 178.2 %all-gather.12.cloned.1.call-start = ((), (), s32[]{:S(2)}) async-start(), calls=%async_computation.10 | async-start | bytes 7077888 | tf_op jit(solution)/shard_map/all_gather | solution.py:121
  104.4 157.2 %all-gather.14.cloned.1.call-start = ((), (), s32[]{:S(2)}) async-start(), calls=%async_computation.11 | async-start | bytes 1474560 | tf_op jit(solution)/shard_map/all_gather | solution.py:99
  105.0 184.3 %all-gather.20.cloned.1.call-start = ((), (), s32[]{:S(2)}) async-start(), calls=%async_computation.14 | async-start | bytes 1474560 | tf_op jit(solution)/shard_map/all_gather | solution.py:102
  105.6 213.4 %all-gather.22.cloned.1.call-start = ((), (), s32[]{:S(2)}) async-start(), calls=%async_computation.15 | async-start | bytes 1474560 | tf_op jit(solution)/shard_map/all_gather | solution.py:104
  106.3 284.7 %all-gather.24.cloned.1.call-start = ((), (), s32[]{:S(2)}) async-start(), calls=%async_computation.16 | async-start | bytes 7864320 | tf_op jit(solution)/shard_map/all_gather | solution.py:106
  107.1 329.8 %all-gather.26.cloned.1.call-start = ((), (), s32[]{:S(2)}) async-start(), calls=%async_computation.17 | async-start | bytes 3932160 | tf_op jit(solution)/shard_map/all_gather | solution.py:107
  107.8 494.1 %reduce-scatter.28.cloned.1.call-start = ((), (), s32[]{:S(2)}) async-start(), calls=%async_computation.25 | async-start | bytes 7077888
  163.8 282.9 %copy-start.77 = (f32[2]{0:T(128)}, f32[2]{0:T(128)S(1)}, u32[]{:S(2)}) copy-start(f32[2]{0:T(128)S(1)} %convert_element_type.209) | copy-start | bytes 28
  163.8 125.5 %copy-start.67 = (f32[768]{0:T(1024)}, f32[768]{0:T(1024)S(1)}, u32[]{:S(2)}) copy-start(f32[768]{0:T(1024)S(1)} %convert_element_type.216) | copy-start | bytes 9220
  263.6 55.3 %copy-start.10 = (f32[2,128,768]{2,1,0:T(8,128)}, f32[2,128,768]{2,1,0:T(8,128)S(1)}, u32[]{:S(2)}) copy-start(f32[2,128,768]{2,1,0:T(8,128)S(1)} %get-tuple-element.472) | copy-start | bytes 2359300
  305.4 92.3 %copy-start.35 = (bf16[2,128,768]{1,2,0:T(8,128)(2,1)}, bf16[2,128,768]{1,2,0:T(8,128)(2,1)S(1)}, u32[]{:S(2)}) copy-start(bf16[2,128,768]{1,2,0:T(8,128)(2,1)S(1)} %get-tuple-element.193) | copy-start | bytes 1179652
  305.4 85.6 %copy-start.55 = (f32[768]{0:T(1024)S(1)}, f32[768]{0:T(1024)}, u32[]{:S(2)}) copy-start(f32[768]{0:T(1024)} %convert_element_type.220) | copy-start | bytes 9220
  320.8 125.6 %copy-start.15 = (f32[2,128,768]{2,1,0:T(8,128)}, f32[2,128,768]{2,1,0:T(8,128)S(1)}, u32[]{:S(2)}) copy-start(f32[2,128,768]{2,1,0:T(8,128)S(1)} %get-tuple-element.474) | copy-start | bytes 2359300
  320.8 125.5 %copy-start.72 = (f32[2,128]{1,0:T(2,128)}, f32[2,128]{1,0:T(2,128)S(1)}, u32[]{:S(2)}) copy-start(f32[2,128]{1,0:T(2,128)S(1)} %fusion.92) | copy-start | bytes 3076
  520.6 151.7 %reduce-scatter.14.cloned.1.call-start = ((), (), s32[]{:S(2)}) async-start(), calls=%async_computation.18 | async-start | bytes 7077888 | tf_op jit(solution)/shard_map/reduce_scatter | solution.py:282
  601.8 109.1 %reduce-scatter.30.cloned.1.call-start = ((), (), s32[]{:S(2)}) async-start(), calls=%async_computation.26 | async-start | bytes 2949120
  612.3 130.7 %reduce-scatter.18.cloned.1.call-start = ((), (), s32[]{:S(2)}) async-start(), calls=%async_computation.20 | async-start | bytes 1474560 | tf_op jit(solution)/shard_map/reduce_scatter | solution.py:317
  614.0 161.0 %reduce-scatter.20.cloned.1.call-start = ((), (), s32[]{:S(2)}) async-start(), calls=%async_computation.21 | async-start | bytes 1474560 | tf_op jit(solution)/shard_map/reduce_scatter | solution.py:326
  616.8 190.1 %reduce-scatter.22.cloned.1.call-start = ((), (), s32[]{:S(2)}) async-start(), calls=%async_computation.22 | async-start | bytes 1474560 | tf_op jit(solution)/shard_map/reduce_scatter | solution.py:332
  618.4 235.8 %reduce-scatter.26.cloned.1.call-start = ((), (), s32[]{:S(2)}) async-start(), calls=%async_computation.24 | async-start | bytes 3932160 | tf_op jit(solution)/shard_map/reduce_scatter | solution.py:341
  622.5 304.8 %reduce-scatter.24.cloned.1.call-start = ((), (), s32[]{:S(2)}) async-start(), calls=%async_computation.23 | async-start | bytes 7864320 | tf_op jit(solution)/shard_map/reduce_scatter | solution.py:338
  628.9 348.7 %reduce-scatter.16.cloned.1.call-start = ((), (), s32[]{:S(2)}) async-start(), calls=%async_computation.19 | async-start | bytes 4423680 | tf_op jit(solution)/shard_map/reduce_scatter | solution.py:314
  676.5 416.6 %all-reduce.17.cloned.1.call-start = ((), (), s32[]{:S(2)}) async-start(), calls=%async_computation.27 | async-start | bytes 9830400 | tf_op jit(solution)/shard_map/psum | solution.py:352
  706.8 271.5 %copy-start.91 = (s32[1024]{0:T(1024)S(1)}, s32[1024]{0:T(1024)}, u32[]{:S(2)}) copy-start(s32[1024]{0:T(1024)} %param.30) | copy-start | bytes 12292
  706.8 272.1 %copy-start.17 = (f32[2,128,768]{2,1,0:T(8,128)S(1)}, f32[2,128,768]{2,1,0:T(8,128)}, u32[]{:S(2)}) copy-start(f32[2,128,768]{2,1,0:T(8,128)} %copy-done.15) | copy-start | bytes 2359300
  706.8 272.2 %copy-start.34 = (bf16[2,128,2048]{2,1,0:T(8,128)(2,1)S(1)}, bf16[2,128,2048]{2,1,0:T(8,128)(2,1)}, u32[]{:S(2)}) copy-start(bf16[2,128,2048]{2,1,0:T(8,128)(2,1)} %get-tuple-element.468) | copy-start | bytes 3145732
  (117 other events, 1056.5 us)
Sparse Core Ops, SparseCore 0:
  9.9 40.1 all-gather.15
  52.0 47.2 all-gather.9
  101.4 64.7 all-gather.17
  168.3 63.3 all-gather.11
  233.4 26.4 all-gather.13
  261.5 27.6 all-gather.19
  291.1 27.7 all-gather.21
  320.8 70.1 all-gather.23
  392.8 43.9 all-gather.25
  520.7 69.7 reduce-scatter.27
  602.0 70.2 reduce-scatter.13
  675.2 35.7 reduce-scatter.29
  714.5 28.5 reduce-scatter.17
  746.4 28.5 reduce-scatter.19
  778.3 28.5 reduce-scatter.21
  810.3 43.9 reduce-scatter.25
  857.1 70.1 reduce-scatter.23
  930.3 47.2 reduce-scatter.15
  980.5 112.5 all-reduce.16
